TPU v7x, 128 devices: a whole 4x4x4 slice. The times are simulated.
128 devices in a mesh: chan: 8 (over x, y_hi), facet: 16 (over y_lo, z, core).
Axes of the slice: x: 4, y: 4 (y_hi: 2, y_lo: 2; y = y_hi * 2 + y_lo), z: 4, core: 2. Of those that a mesh axis runs over, the one named last changes fastest.
Arguments:
- image: float32 [8, 2048, 2048], P(None, 'facet', 'chan'), may hold values from 0 to 1
- lowrank_dual: float32 [8, 2048, 2048], P(None, 'facet', 'chan'), may hold values from -6 to 6
- wavelet_dual: float32 [8, 4096, 4096], P(None, 'facet', 'chan'), may hold values from -6 to 6
- data_dual: float32 [2, 8, 512, 2048], P(None, 'chan', None, 'facet'), may hold values from -6 to 6
- observed: float32 [2, 8, 512, 2048], P(None, 'chan', None, 'facet'), may hold values from -6 to 6
- kernel_weights: bfloat16 [8, 512, 2048], P('chan', None, 'facet'), may hold values from 0.25 to 2
- analysis_matrix: bfloat16 [256, 256], replicated, may hold values from -0.375 to 0.375
- block_rows: int32 [8, 16, 4], P('chan', 'facet'), may hold values from 0 to 15, as said below
- intersection_widths: int32 [16, 16], P('facet', 'chan'), may hold values from 16 to 64
- ball_radii: float32 [8, 16], P('chan', 'facet'), may hold values from 230.4 to 614.4
Outputs:
- image_next: float32 [8, 2048, 2048], P(None, 'facet', 'chan')
- lowrank_next: float32 [8, 2048, 2048], P(None, 'facet', 'chan')
- wavelet_next: float32 [8, 4096, 4096], P(None, 'facet', 'chan')
- data_next: float32 [2, 8, 512, 2048], P(None, 'chan', None, 'facet')
Inputs may be any that keep to these rules, and one draw needn't show every extreme that they name: `block_rows`: for each channel and column block the 4 row blocks are distinct.
All inputs are finite; a program needn't handle non-finite values.
Results may differ from a plain program's by a relative error of at most 0.0062.
Values may be sent and summed in bfloat16 or wider, within the bound.
A program may use at most 128 MiB of HBM per device.

v0:
```python
import math
from functools import partial

import jax
import jax.numpy as jnp
import ml_dtypes
import numpy as np
from jax import lax
from jax.experimental import pallas as pl
from jax.experimental.pallas import tpu as pltpu
from jax.sharding import PartitionSpec as P

N = 2048
FS = 128
HALO = 64
E = 256
BLK = 128
R = 4
C = 8
NB = 16
CHUNKS = 4
ROWS = N // CHUNKS

step_size = 0.5
clip_bound = 1.5
shrink_ratio = 0.5
tiny_value = 1e-06

MESH = pl.DeviceIdType.MESH
f32 = jnp.float32
bf16 = jnp.bfloat16


def dft_table():
    index = np.arange(N, dtype=np.int64)
    angle = (index[:, None] * index[None, :] % N) * (2.0 * math.pi / N)
    scale = 1.0 / math.sqrt(N)
    parts = np.stack([np.cos(angle) * scale, -np.sin(angle) * scale])
    return (
        parts.reshape(2, N, NB, BLK)
        .transpose(1, 2, 0, 3)
        .reshape(N, 2 * N)
        .astype(ml_dtypes.bfloat16)
    )


def dot(a, b):
    return lax.dot_general(a, b, (((1,), (0,)), ((), ())), preferred_element_type=f32)


def dot_nt(a, b):
    return lax.dot_general(a, b, (((1,), (1,)), ((), ())), preferred_element_type=f32)


def swap_halves(x):
    return pltpu.roll(x, HALO, 1)


def lane_low(shape):
    return lax.broadcasted_iota(jnp.int32, shape, 1) < HALO


def facet_masks(width, up, down, left, right):
    row = lax.broadcasted_iota(jnp.int32, (E, FS), 0)
    away = jnp.maximum(jnp.maximum(HALO - row, row - (HALO + FS - 1)), 0)
    rows_in = (away <= width) & ((row >= HALO) | up) & ((row < HALO + FS) | down)
    lane = lax.broadcasted_iota(jnp.int32, (E, FS), 1)
    low = lane < HALO
    away = jnp.where(low, lane + 1, FS - lane)
    lanes_in = (away <= width) & ((low & right) | (jnp.logical_not(low) & left))
    return rows_in, rows_in & lanes_in


def body(
    rows_ref,
    widths_ref,
    radii_ref,
    matrix_ref,
    image_hbm,
    lowrank_hbm,
    wavelet_hbm,
    dual_hbm,
    observed_hbm,
    weights_hbm,
    table_hbm,
    image_out,
    lowrank_out,
    wavelet_out,
    data_out,
    t0,
    t1,
    t2,
    t3,
    first_columns,
    first_rows,
    phases,
    wav,
    img,
    low,
    dual,
    obs,
    wgt,
    weighted,
    spread,
    rows_back,
    acc,
    adj_send,
    adj_recv,
    turned,
    rolled,
    syn,
    syn_left,
    syn_right,
    center,
    from_up,
    from_down,
    from_left,
    from_left_corner,
    from_right,
    from_right_corner,
    padded,
    edge_left,
    edge_right,
    halo_left,
    halo_right,
    regrouped,
    spec,
    spec_recv,
    forward,
    gram,
    shrink,
    low_next,
    table_sem,
    wav_sem,
    in_sem,
    out_sem,
    wav_out_sem,
    low_out_sem,
    a1s,
    a1r,
    a2s,
    a2r,
    a3s,
    a3r,
    a4s,
    a4r,
    h1s,
    h1r,
    h2s,
    h2r,
):
    tables = (t0, t1, t2, t3)
    c = lax.axis_index("chan")
    p = lax.axis_index("facet")
    up, down = lax.rem(p + NB - 1, NB), lax.rem(p + 1, NB)
    left, right = lax.rem(c + C - 1, C), lax.rem(c + 1, C)
    group = p // (NB // CHUNKS)
    held = [lax.rem(group + t, CHUNKS) for t in range(CHUNKS)]

    small = [
        pltpu.make_async_copy(src, dst, in_sem.at[k])
        for k, (src, dst) in enumerate(
            (
                (dual_hbm, dual),
                (weights_hbm, wgt),
                (image_hbm, img),
                (lowrank_hbm, low),
                (observed_hbm, obs),
            )
        )
    ]
    small[0].start()
    small[1].start()
    column_copy = pltpu.make_async_copy(
        table_hbm.at[pl.ds(0, N), pl.ds(0, E)], first_columns, in_sem.at[5]
    )
    column_copy.start()
    row_copy = pltpu.make_async_copy(table_hbm.at[pl.ds(0, BLK)], first_rows, in_sem.at[6])
    table_copies = []
    for t in range(CHUNKS):
        start = pl.multiple_of(held[t] * ROWS, ROWS)
        copy = pltpu.make_async_copy(table_hbm.at[pl.ds(start, ROWS)], tables[t], table_sem.at[t])
        copy.start()
        table_copies.append(copy)
    for k in range(C):
        pltpu.make_async_copy(wavelet_hbm.at[k], wav.at[k], wav_sem.at[k]).start()
    for k in range(2, 5):
        small[k].start()
    row_copy.start()

    barrier = pltpu.get_barrier_semaphore()

    def greet_facet(s, carry):
        peer = lax.rem(p + s, NB)
        pl.semaphore_signal(barrier, inc=1, device_id=(c, peer), device_id_type=MESH)
        return carry

    def greet_chan(s, carry):
        peer = lax.rem(c + s, C)
        pl.semaphore_signal(barrier, inc=1, device_id=(peer, p), device_id_type=MESH)
        return carry

    lax.fori_loop(1, NB, greet_facet, 0)
    lax.fori_loop(1, C, greet_chan, 0)
    for a in (left, right):
        for b in (up, down):
            pl.semaphore_signal(barrier, inc=1, device_id=(a, b), device_id_type=MESH)

    matrix = matrix_ref[...]
    turned[...] = matrix.astype(f32).T.astype(bf16)
    rolled[...] = pltpu.roll(matrix.astype(f32), E - HALO, 1).astype(bf16)

    row16 = lax.broadcasted_iota(jnp.int32, (NB, BLK), 0)
    for q in range(R):
        turn = (rows_ref[0, 0, q] * row16) & (NB - 1)
        cosine, sine = jnp.zeros((NB, BLK), f32), jnp.zeros((NB, BLK), f32)
        for m in range(NB):
            cosine = jnp.where(turn == m, math.cos(2.0 * math.pi * m / NB), cosine)
            sine = jnp.where(turn == m, math.sin(2.0 * math.pi * m / NB), sine)
        phases[q, 0] = cosine
        phases[q, 1] = sine

    small[0].wait()
    small[1].wait()
    for q in range(R):
        span = slice(q * BLK, (q + 1) * BLK)
        weight = wgt[span, :].astype(f32)
        real = (dual[0, span, :] * weight).astype(bf16)
        imag = (dual[1, span, :] * weight).astype(bf16)
        lanes_real = slice(q * E, q * E + BLK)
        lanes_imag = slice(q * E + BLK, (q + 1) * E)
        weighted[:BLK, lanes_real] = real
        weighted[:BLK, lanes_imag] = imag
        weighted[BLK:, lanes_real] = imag
        weighted[BLK:, lanes_imag] = -real

    def remote(src, dst, send, recv, chan, facet):
        return pltpu.make_async_remote_copy(
            src_ref=src,
            dst_ref=dst,
            send_sem=send,
            recv_sem=recv,
            device_id=(chan, facet),
            device_id_type=MESH,
        )

    column_copy.wait()
    pl.semaphore_wait(barrier, NB - 1 + C - 1 + 4)

    def spread_pair(s, carry):
        pair = lax.rem(p // 2 + s, NB // 2)
        start = pl.multiple_of(pair * 2 * FS, 2 * FS)
        out = dot(first_columns[pl.ds(start, 2 * FS), :], weighted[...])
        real, imag = None, None
        for q in range(R):
            part_real = out[:, q * E : q * E + BLK].reshape(16, NB, BLK)
            part_imag = out[:, q * E + BLK : (q + 1) * E].reshape(16, NB, BLK)
            cosine, sine = phases[q, 0][None], phases[q, 1][None]
            term_real = cosine * part_real - sine * part_imag
            term_imag = cosine * part_imag + sine * part_real
            real = term_real if real is None else real + term_real
            imag = term_imag if imag is None else imag + term_imag
        rounded = jnp.concatenate(
            [real.reshape(2 * FS, BLK), imag.reshape(2 * FS, BLK)], axis=1
        ).astype(bf16)
        for k in range(2):
            target = pair * 2 + k
            block = rounded[k * FS : (k + 1) * FS]
            spread[target] = block

            @pl.when(target != p)
            def _():
                remote(
                    spread.at[target], rows_back.at[p], a1s.at[target], a1r.at[p], c, target
                ).start()

            @pl.when(target == p)
            def _():
                rows_back[p] = block

        return carry

    lax.fori_loop(1, NB // 2 + 1, spread_pair, 0)

    is_low = lane_low((E, FS))
    valid_up, valid_down = p > 0, p < NB - 1
    valid_left, valid_right = c > 0, c < C - 1

    def synth_channel(k, masks):
        pltpu.make_async_copy(wavelet_hbm.at[k], wav.at[k], wav_sem.at[k]).wait()
        half = dot(turned[...], wav[k].astype(bf16)).astype(bf16)
        cores, margins = [], []
        for f in range(2):
            out = dot(half[:, f * E : (f + 1) * E], rolled[...])
            rows_in, both = masks[f]
            cores.append(jnp.where(rows_in, out[:, :FS], 0.0))
            margins.append(jnp.where(both, out[:, FS:], 0.0))
        tile0 = cores[0] + jnp.where(is_low, 0.0, margins[1])
        tile1 = cores[1] + jnp.where(is_low, margins[0], 0.0)
        syn[k, :, :FS] = tile0.astype(bf16)
        syn[k, :, FS:] = tile1.astype(bf16)
        center[k, :, :FS] = tile0[HALO : HALO + FS]
        center[k, :, FS:] = tile1[HALO : HALO + FS]
        return margins

    true = p >= 0

    def synth_pair(k, carry):
        masks = [facet_masks(widths_ref[0, f], true, true, true, true) for f in range(2)]
        first = synth_channel(k, masks)
        second = synth_channel(k + 4, masks)
        syn_left[k] = jnp.where(is_low, swap_halves(second[0]), first[0]).astype(bf16)
        syn_right[k] = jnp.where(is_low, first[1], swap_halves(second[1])).astype(bf16)
        return carry

    lax.fori_loop(0, 4, synth_pair, 0)

    top, mid, bottom = pl.ds(0, HALO), pl.ds(HALO, FS), pl.ds(HALO + FS, HALO)
    first_half, second_half = pl.ds(0, HALO), pl.ds(HALO, HALO)
    every = slice(None)
    margin_copies = [
        remote(src, dst, h1s.at[k], h1r.at[k], a, b)
        for k, (src, dst, a, b) in enumerate(
            (
                (syn.at[every, top], from_down, c, up),
                (syn.at[every, bottom], from_up, c, down),
                (syn_left.at[every, mid], from_right, left, p),
                (syn_right.at[every, mid], from_left, right, p),
                (syn_left.at[every, top], from_right_corner.at[every, second_half], left, up),
                (syn_left.at[every, bottom], from_right_corner.at[every, first_half], left, down),
                (syn_right.at[every, top], from_left_corner.at[every, second_half], right, up),
                (syn_right.at[every, bottom], from_left_corner.at[every, first_half], right, down),
            )
        )
    ]
    for copy in margin_copies:
        copy.start()

    acc[...] = jnp.zeros_like(acc)
    for copy in table_copies:
        copy.wait()

    def back_block(s, carry):
        j = lax.rem(p + s, NB)

        @pl.when(s > 0)
        def _():
            remote(rows_back.at[j], rows_back.at[j], a1s.at[j], a1r.at[j], c, j).wait_recv()

        block = rows_back[j]
        start = pl.multiple_of(j * E, E)
        for t in range(CHUNKS):
            acc[t] += dot_nt(block, tables[t][:, pl.ds(start, E)])
        return carry

    lax.fori_loop(0, NB, back_block, 0)

    for t in range(CHUNKS):
        for k in range(2):
            target = held[t] * 2 + k
            adj_send[2 * t + k] = acc[t, :, k * E : (k + 1) * E].astype(bf16)

            @pl.when(target != c)
            def _():
                remote(
                    adj_send.at[2 * t + k], adj_recv.at[c], a2s.at[target], a2r.at[c], target, p
                ).start()

            @pl.when(target == c)
            def _():
                adj_recv[c] = adj_send[2 * t + k]

    small[2].wait()
    small[3].wait()
    small[4].wait()
    for copy in margin_copies:
        copy.wait_recv()
    half_low = lane_low((FS, FS))
    zero = jnp.zeros((), f32)

    def gather_prior(k, carry):
        pair = lax.rem(k, 4)
        is_first = k < 4
        row = lax.broadcasted_iota(jnp.int32, (FS, FS), 0)
        corner_ok = ((row < HALO) & valid_up) | ((row >= HALO) & valid_down)
        sides = from_left[pair].astype(f32) + jnp.where(
            corner_ok, from_left_corner[pair].astype(f32), 0.0
        )
        sides = jnp.where(is_first, sides, swap_halves(sides))
        tile0 = jnp.where(half_low & valid_left, sides, 0.0)
        sides = from_right[pair].astype(f32) + jnp.where(
            corner_ok, from_right_corner[pair].astype(f32), 0.0
        )
        sides = jnp.where(is_first, sides, swap_halves(sides))
        tile1 = jnp.where(jnp.logical_not(half_low) & valid_right, sides, 0.0)
        above = jnp.where(valid_up, from_up[k].astype(f32), 0.0)
        below = jnp.where(valid_down, from_down[k].astype(f32), 0.0)
        sides = jnp.concatenate([tile0, tile1], axis=1)
        vertical = jnp.concatenate([above, below], axis=0)
        prior = center[k] + sides + vertical
        center[k] = img[k] - step_size * (prior + low[k])
        return carry

    lax.fori_loop(0, C, gather_prior, 0)

    def image_step(s, carry):
        k = lax.rem(c + s, C)

        @pl.when(s > 0)
        def _():
            remote(adj_recv.at[k], adj_recv.at[k], a2s.at[k], a2r.at[k], k, p).wait_recv()

        updated = jnp.maximum(center[k] - step_size * adj_recv[k].astype(f32), 0.0)
        tilde = 2.0 * updated - img[k]
        center[k] = updated
        padded[k, HALO : HALO + FS, :] = tilde.astype(bf16)
        low[k] = low[k] + tilde

        @pl.when(s > 0)
        def _():
            remote(
                padded.at[k, mid], regrouped.at[c], a3s.at[k], a3r.at[c], k, p
            ).start()

        @pl.when(s == 0)
        def _():
            regrouped[c] = tilde.astype(bf16)

        return carry

    lax.fori_loop(0, C, image_step, 0)
    image_copy = pltpu.make_async_copy(center, image_out, out_sem.at[0])
    image_copy.start()

    def pack_edges(k, carry):
        first = padded[k, HALO : HALO + FS, :].astype(f32)
        second = padded[k + 4, HALO : HALO + FS, :].astype(f32)
        edge_right[k] = jnp.where(
            half_low, swap_halves(second[:, FS:]), first[:, FS:]
        ).astype(bf16)
        edge_left[k] = jnp.where(
            half_low, first[:, :FS], swap_halves(second[:, :FS])
        ).astype(bf16)
        return carry

    lax.fori_loop(0, 4, pack_edges, 0)
    upper, lower = pl.ds(HALO, HALO), pl.ds(FS, HALO)
    halo_copies = [
        remote(src, dst, h2s.at[k], h2r.at[k], a, b)
        for k, (src, dst, a, b) in enumerate(
            (
                (padded.at[every, upper], padded.at[every, bottom], c, up),
                (padded.at[every, lower], padded.at[every, top], c, down),
                (edge_left, halo_right.at[every, mid], left, p),
                (edge_right, halo_left.at[every, mid], right, p),
                (edge_left.at[every, first_half], halo_right.at[every, bottom], left, up),
                (edge_left.at[every, second_half], halo_right.at[every, top], left, down),
                (edge_right.at[every, first_half], halo_left.at[every, bottom], right, up),
                (edge_right.at[every, second_half], halo_left.at[every, top], right, down),
            )
        )
    ]
    for copy in halo_copies:
        copy.start()

    for f in range(2):
        lanes = slice(f * FS, (f + 1) * FS)

        def gram_row(a, carry):
            mine = low[a, :, lanes].astype(bf16).astype(f32)
            for b in range(C):
                other = low[b, :, lanes].astype(bf16).astype(f32)
                gram[a, b : b + 1, :] = jnp.sum(mine * other, axis=0, keepdims=True)
            return carry

        lax.fori_loop(0, C, gram_row, 0)
        total = jnp.sum(gram[...], axis=2)
        row = lax.broadcasted_iota(jnp.int32, (C, C), 0)
        col = lax.broadcasted_iota(jnp.int32, (C, C), 1)
        eye = (row == col).astype(f32)
        trace = jnp.sum(jnp.sum(total * eye, axis=1, keepdims=True), axis=0, keepdims=True)
        ridge = shrink_ratio * (trace / C + tiny_value)
        system = total + ridge * eye
        inverse = eye
        for k in range(C):
            pivot = 1.0 / system[k : k + 1, k : k + 1]
            row_s = system[k : k + 1, :] * pivot
            row_i = inverse[k : k + 1, :] * pivot
            column = jnp.where(row == k, 0.0, jnp.broadcast_to(system[:, k : k + 1], (C, C)))
            system = jnp.where(row == k, jnp.broadcast_to(row_s, (C, C)), system - column * row_s)
            inverse = jnp.where(row == k, jnp.broadcast_to(row_i, (C, C)), inverse - column * row_i)
        inverse = ridge * inverse
        for k in range(C):
            shrink[k] = jnp.broadcast_to(inverse[:, k : k + 1], (C, FS))

        def apply_row(r, carry):
            span = pl.ds(pl.multiple_of(r * 16, 16), 16)
            blocks = [low[b, span, lanes] for b in range(C)]
            for a in range(C):
                out = None
                for b in range(C):
                    term = shrink[b, a : a + 1, :] * blocks[b]
                    out = term if out is None else out + term
                low_next[a, span, lanes] = out
            return carry

        lax.fori_loop(0, FS // 16, apply_row, 0)
    low_copy = pltpu.make_async_copy(low_next, lowrank_out, low_out_sem.at[0])
    low_copy.start()

    def arrive(s, carry):
        k = lax.rem(c + s, C)
        remote(regrouped.at[k], regrouped.at[k], a3s.at[k], a3r.at[k], k, p).wait_recv()
        return carry

    lax.fori_loop(1, C, arrive, 0)

    def spectrum_block(s, carry):
        j = lax.rem(p + s, NB)
        start = pl.multiple_of(j * E, E)
        total = None
        for t in range(CHUNKS):
            for k in range(2):
                term = dot(regrouped[held[t] * 2 + k], tables[t][k * E : (k + 1) * E, pl.ds(start, E)])
                total = term if total is None else total + term
        spec[j] = total.astype(bf16)

        @pl.when(s < NB)
        def _():
            remote(spec.at[j], spec_recv.at[p], a4s.at[j], a4r.at[p], c, j).start()

        @pl.when(s == NB)
        def _():
            spec_recv[p] = total.astype(bf16)

        return carry

    lax.fori_loop(1, NB + 1, spectrum_block, 0)

    for copy in halo_copies:
        copy.wait_recv()

    def analysis(k, carry):
        pair = lax.rem(k, 4)
        is_first = k < 4
        tiles = padded[k].astype(f32)
        tile0, tile1 = tiles[:, :FS], tiles[:, FS:]
        side = halo_left[pair].astype(f32)
        beside_left = jnp.where(is_first, side, swap_halves(side))
        side = halo_right[pair].astype(f32)
        beside_right = jnp.where(is_first, side, swap_halves(side))
        margins = (
            jnp.where(is_low, tile1, beside_left),
            jnp.where(is_low, beside_right, tile0),
        )
        for f in range(2):
            rows_in, both = facet_masks(
                widths_ref[0, f],
                valid_up,
                valid_down,
                valid_left if f == 0 else true,
                valid_right if f == 1 else true,
            )
            core = jnp.where(rows_in, tile0 if f == 0 else tile1, 0.0)
            margin = jnp.where(both, margins[f], 0.0)
            piece = jnp.concatenate([core, margin], axis=1).astype(bf16)
            half = dot(matrix_ref[...], piece).astype(bf16)
            coefficients = dot_nt(half, rolled[...])
            lanes = slice(f * E, (f + 1) * E)
            wav[k, :, lanes] = jnp.clip(wav[k, :, lanes] + coefficients, -clip_bound, clip_bound)
        pltpu.make_async_copy(wav.at[k], wavelet_out.at[k], wav_out_sem.at[k]).start()
        return carry

    lax.fori_loop(0, C, analysis, 0)

    forward[...] = jnp.zeros_like(forward)
    row_copy.wait()

    def forward_block(s, carry):
        j = lax.rem(p + s, NB)

        @pl.when(s > 0)
        def _():
            remote(spec_recv.at[j], spec_recv.at[j], a4s.at[j], a4r.at[j], c, j).wait_recv()

        block = spec_recv[j].astype(f32)
        real = block[:, :BLK].reshape(FS // NB, NB, BLK)
        imag = block[:, BLK:].reshape(FS // NB, NB, BLK)
        start = pl.multiple_of(j * E, E)
        rows_table = first_rows[:, pl.ds(start, E)]
        for q in range(R):
            cosine, sine = phases[q, 0][None], phases[q, 1][None]
            turned_real = (cosine * real + sine * imag).reshape(FS, BLK)
            turned_imag = (cosine * imag - sine * real).reshape(FS, BLK)
            upper_rows = jnp.concatenate([turned_real, turned_imag], axis=1)
            lower_rows = jnp.concatenate([-turned_imag, turned_real], axis=1)
            both = jnp.concatenate([upper_rows, lower_rows], axis=0).astype(bf16)
            forward[q * BLK : (q + 1) * BLK, :] += dot(rows_table, both)
        return carry

    lax.fori_loop(0, NB, forward_block, 0)

    weight = wgt[...].astype(f32)
    squares = jnp.zeros((1, BLK), f32)
    for part in range(2):
        residual = dual[part] + weight * forward[:, part * BLK : (part + 1) * BLK] - obs[part]
        dual[part] = residual
        squares = squares + jnp.sum(residual * residual, axis=0, keepdims=True)
    norm = jnp.sqrt(jnp.sum(squares, axis=1, keepdims=True))
    radius = radii_ref[0, 0]
    factor = jnp.maximum(0.0, 1.0 - radius / jnp.maximum(norm, radius))
    for part in range(2):
        dual[part] = dual[part] * factor
    data_copy = pltpu.make_async_copy(dual, data_out, out_sem.at[1])
    data_copy.start()

    def end_facet(s, carry):
        j = lax.rem(p + s, NB)
        remote(spec.at[j], spec_recv.at[j], a1s.at[j], a1r.at[j], c, j).wait_send()
        remote(spec.at[j], spec_recv.at[j], a4s.at[j], a4r.at[j], c, j).wait_send()
        return carry

    def end_chan(s, carry):
        k = lax.rem(c + s, C)
        remote(adj_send.at[k], adj_recv.at[k], a2s.at[k], a2r.at[k], k, p).wait_send()
        remote(padded.at[k, mid], regrouped.at[k], a3s.at[k], a3r.at[k], k, p).wait_send()
        return carry

    lax.fori_loop(1, NB, end_facet, 0)
    lax.fori_loop(1, C, end_chan, 0)
    for copy in margin_copies + halo_copies:
        copy.wait_send()
    image_copy.wait()
    low_copy.wait()

    def end_wavelet(k, carry):
        pltpu.make_async_copy(wav.at[k], wavelet_out.at[k], wav_out_sem.at[k]).wait()
        return carry

    lax.fori_loop(0, C, end_wavelet, 0)
    data_copy.wait()


def shards(
    image,
    lowrank_dual,
    wavelet_dual,
    data_dual,
    observed,
    kernel_weights,
    analysis_matrix,
    block_rows,
    intersection_widths,
    ball_radii,
):
    rows = R * BLK
    vmem = pltpu.VMEM
    dma = pltpu.SemaphoreType.DMA
    scratch = (
        [vmem((ROWS, 2 * N), bf16)] * 4
        + [
            vmem((N, E), bf16),
            vmem((BLK, 2 * N), bf16),
            vmem((R, 2, NB, BLK), f32),
            vmem((C, E, 2 * E), f32),
            vmem((C, FS, E), f32),
            vmem((C, FS, E), f32),
            vmem((2, rows, BLK), f32),
            vmem((2, rows, BLK), f32),
            vmem((rows, BLK), bf16),
            vmem((E, R * E), bf16),
            vmem((NB, FS, E), bf16),
            vmem((NB, FS, E), bf16),
            vmem((CHUNKS, FS, ROWS), f32),
            vmem((C, FS, E), bf16),
            vmem((C, FS, E), bf16),
            vmem((E, E), bf16),
            vmem((E, E), bf16),
            vmem((C, E, E), bf16),
            vmem((4, E, FS), bf16),
            vmem((4, E, FS), bf16),
            vmem((C, FS, E), f32),
            vmem((C, HALO, E), bf16),
            vmem((C, HALO, E), bf16),
            vmem((4, FS, FS), bf16),
            vmem((4, FS, FS), bf16),
            vmem((4, FS, FS), bf16),
            vmem((4, FS, FS), bf16),
            vmem((C, E, E), bf16),
            vmem((4, FS, FS), bf16),
            vmem((4, FS, FS), bf16),
            vmem((4, E, FS), bf16),
            vmem((4, E, FS), bf16),
            vmem((C, FS, E), bf16),
            vmem((NB, FS, E), bf16),
            vmem((NB, FS, E), bf16),
            vmem((rows, E), f32),
            vmem((C, C, FS), f32),
            vmem((C, C, FS), f32),
            vmem((C, FS, E), f32),
        ]
        + [dma((n,)) for n in (4, 8, 7, 2, 8, 1, 16, 16, 8, 8, 8, 8, 16, 16, 8, 8, 8, 8)]
    )
    hbm = pl.BlockSpec(memory_space=pl.ANY)
    smem = pl.BlockSpec(memory_space=pltpu.SMEM)
    image_next, lowrank_next, wavelet_next, data_next = pl.pallas_call(
        body,
        out_shape=(
            jax.ShapeDtypeStruct((C, FS, E), f32),
            jax.ShapeDtypeStruct((C, FS, E), f32),
            jax.ShapeDtypeStruct((C, E, 2 * E), f32),
            jax.ShapeDtypeStruct((2, rows, BLK), f32),
        ),
        in_specs=[smem] * 3 + [pl.BlockSpec(memory_space=pltpu.VMEM)] + [hbm] * 7,
        out_specs=(hbm,) * 4,
        scratch_shapes=scratch,
        compiler_params=pltpu.CompilerParams(
            collective_id=0, has_side_effects=True, vmem_limit_bytes=60 * 1024 * 1024
        ),
    )(
        block_rows,
        intersection_widths,
        ball_radii,
        analysis_matrix,
        image,
        lowrank_dual,
        wavelet_dual,
        data_dual.reshape(2, rows, BLK),
        observed.reshape(2, rows, BLK),
        kernel_weights.reshape(rows, BLK),
        jnp.asarray(dft_table()),
    )
    return image_next, lowrank_next, wavelet_next, data_next.reshape(2, 1, rows, BLK)


def solution(mesh):
    in_specs = (
        P(None, "facet", "chan"),
        P(None, "facet", "chan"),
        P(None, "facet", "chan"),
        P(None, "chan", None, "facet"),
        P(None, "chan", None, "facet"),
        P("chan", None, "facet"),
        P(),
        P("chan", "facet", None),
        P("facet", "chan"),
        P("chan", "facet"),
    )
    out_specs = (
        P(None, "facet", "chan"),
        P(None, "facet", "chan"),
        P(None, "facet", "chan"),
        P(None, "chan", None, "facet"),
    )
    return jax.shard_map(shards, mesh=mesh, in_specs=in_specs, out_specs=out_specs, check_vma=False)
```

profile of v0, /device:TPU:97, one launch (start us, length us, event | category | flops | bytes accessed | tf_op | source)
XLA Modules:
  0.0 90.1 jit_solution(3829469645500862358)
XLA Ops:
  1.3 81.3 %shard_map.138 = (f32[8,128,256]{2,1,0:T(8,128)}, f32[8,128,256]{2,1,0:T(8,128)}, f32[8,256,512]{2,1,0:T(8,128)}, f32[2,512,128]{2,1,0:T(8,128)}) custom-call(s32[1,1,4]{2,1,0:T(1,128)} %rows_ref.1, s32[1,2]{1,0:T(1,128)} %widths_ref.1, f32[1,1]{1,0:T(1,128)S(6)} %copy.20.radii_ref, bf16[256,256]{1,0:T(8,128)(2,1)} %matrix_ref.1, f32[8,128,256]{2,1,0:T(8,128)} %image_hbm.1, ...), custom_call_target="tpu_custom_call" | custom-call | tf_op jit(solution)/shard_map/pallas_call | solution.py:706
  82.5 0.0 copy-start
  82.5 2.4 %copy.21 = f32[8,128,256]{2,1,0:T(8,128)} copy(f32[8,128,256]{2,1,0:T(8,128)} %get-tuple-element.20) | data formatting | bytes 2097152
  85.0 2.3 %copy.22 = f32[8,128,256]{2,1,0:T(8,128)} copy(f32[8,128,256]{2,1,0:T(8,128)} %get-tuple-element.21) | data formatting | bytes 2097152
  87.2 0.0 copy-done
  87.2 0.0 copy-start.1
  87.2 2.0 %copy.23 = f32[8,256,512]{2,1,0:T(8,128)} copy(f32[8,256,512]{2,1,0:T(8,128)S(1)} %copy-done) | data formatting | bytes 8388608
  89.3 0.0 copy-done.1
  89.3 0.8 copy.24
Async XLA Ops:
  82.5 4.7 %copy-start = (f32[8,256,512]{2,1,0:T(8,128)S(1)}, f32[8,256,512]{2,1,0:T(8,128)}, u32[]{:S(2)}) copy-start(f32[8,256,512]{2,1,0:T(8,128)} %get-tuple-element.22) | copy-start | bytes 12582916
  87.2 2.0 %copy-start.1 = (f32[2,512,128]{2,1,0:T(8,128)S(1)}, f32[2,512,128]{2,1,0:T(8,128)}, u32[]{:S(2)}) copy-start(f32[2,512,128]{2,1,0:T(8,128)} %get-tuple-element.11) | copy-start | bytes 1572868
where the time goes:
time: 90.2 us; the launch traced here: 90.1 us
  Pallas kernels  81.3 us (90%)
  local copies, waits for them, and re-layouts  7.5 us (8%)
  between operations  1.3 us (1%)
    pallas_call x1, Pallas kernels, shards(): pl.pallas_call(body, out_shape=(jax.ShapeDtypeStruct((C, FS, E), f32), ja...  81.3 us
    unnamed x8, local copies, waits for them, and re-layouts  7.5 us

commit v1 on v0

--- a/solution.py
+++ b/solution.py
@@ -20,6 +20,9 @@
 NB = 16
 CHUNKS = 4
 ROWS = N // CHUNKS
+HALVES = 2
+GROUP = 4
+HR = FS // HALVES
 
 step_size = 0.5
 clip_bound = 1.5
@@ -40,6 +43,23 @@
         parts.reshape(2, N, NB, BLK)
         .transpose(1, 2, 0, 3)
         .reshape(N, 2 * N)
+        .astype(ml_dtypes.bfloat16)
+    )
+
+
+def turned_table():
+    return np.ascontiguousarray(dft_table().T)
+
+
+def first_row_table():
+    index = np.arange(N, dtype=np.int64)
+    angle = (np.arange(BLK, dtype=np.int64)[:, None] * index[None, :] % N) * (2.0 * math.pi / N)
+    scale = 1.0 / math.sqrt(N)
+    parts = np.stack([np.cos(angle) * scale, -np.sin(angle) * scale])
+    return (
+        parts.reshape(2, BLK, NB // HALVES, HALVES, HALVES, HR)
+        .transpose(1, 2, 4, 0, 3, 5)
+        .reshape(BLK, 2 * N)
         .astype(ml_dtypes.bfloat16)
     )
 
@@ -83,6 +103,8 @@
     observed_hbm,
     weights_hbm,
     table_hbm,
+    row_table_hbm,
+    turned_hbm,
     image_out,
     lowrank_out,
     wavelet_out,
@@ -91,6 +113,7 @@
     t1,
     t2,
     t3,
+    turned_rows,
     first_columns,
     first_rows,
     phases,
@@ -114,10 +137,14 @@
     center,
     from_up,
     from_down,
+    from_up_left,
+    from_up_right,
+    from_down_left,
+    from_down_right,
+    fold_left,
+    fold_right,
     from_left,
-    from_left_corner,
     from_right,
-    from_right_corner,
     padded,
     edge_left,
     edge_right,
@@ -131,6 +158,7 @@
     shrink,
     low_next,
     table_sem,
+    turned_sem,
     wav_sem,
     in_sem,
     out_sem,
@@ -154,8 +182,6 @@
     p = lax.axis_index("facet")
     up, down = lax.rem(p + NB - 1, NB), lax.rem(p + 1, NB)
     left, right = lax.rem(c + C - 1, C), lax.rem(c + 1, C)
-    group = p // (NB // CHUNKS)
-    held = [lax.rem(group + t, CHUNKS) for t in range(CHUNKS)]
 
     small = [
         pltpu.make_async_copy(src, dst, in_sem.at[k])
@@ -175,18 +201,20 @@
         table_hbm.at[pl.ds(0, N), pl.ds(0, E)], first_columns, in_sem.at[5]
     )
     column_copy.start()
-    row_copy = pltpu.make_async_copy(table_hbm.at[pl.ds(0, BLK)], first_rows, in_sem.at[6])
+    row_copy = pltpu.make_async_copy(row_table_hbm, first_rows, in_sem.at[6])
     table_copies = []
     for t in range(CHUNKS):
-        start = pl.multiple_of(held[t] * ROWS, ROWS)
-        copy = pltpu.make_async_copy(table_hbm.at[pl.ds(start, ROWS)], tables[t], table_sem.at[t])
-        copy.start()
+        copy = pltpu.make_async_copy(
+            table_hbm.at[pl.ds(t * ROWS, ROWS)], tables[t], table_sem.at[t]
+        )
         table_copies.append(copy)
-    for k in range(C):
-        pltpu.make_async_copy(wavelet_hbm.at[k], wav.at[k], wav_sem.at[k]).start()
-    for k in range(2, 5):
-        small[k].start()
-    row_copy.start()
+    turned_copies = []
+    for t in range(NB // GROUP):
+        start = lax.rem(p // GROUP + t, NB // GROUP) * GROUP * E
+        span = pl.ds(pl.multiple_of(start, GROUP * E), GROUP * E)
+        turned_copies.append(
+            pltpu.make_async_copy(turned_hbm.at[span], turned_rows.at[span], turned_sem.at[t])
+        )
 
     barrier = pltpu.get_barrier_semaphore()
 
@@ -202,9 +230,6 @@
 
     lax.fori_loop(1, NB, greet_facet, 0)
     lax.fori_loop(1, C, greet_chan, 0)
-    for a in (left, right):
-        for b in (up, down):
-            pl.semaphore_signal(barrier, inc=1, device_id=(a, b), device_id_type=MESH)
 
     matrix = matrix_ref[...]
     turned[...] = matrix.astype(f32).T.astype(bf16)
@@ -245,7 +270,26 @@
         )
 
     column_copy.wait()
-    pl.semaphore_wait(barrier, NB - 1 + C - 1 + 4)
+    for k in range(C):
+        pltpu.make_async_copy(wavelet_hbm.at[k], wav.at[k], wav_sem.at[k]).start()
+    for copy in turned_copies:
+        copy.start()
+    for k in range(2, 5):
+        small[k].start()
+    for copy in table_copies:
+        copy.start()
+    row_copy.start()
+    pl.semaphore_wait(barrier, NB - 1 + C - 1)
+
+    def send_rows(target, half):
+        remote(
+            spread.at[target, half],
+            rows_back.at[p, half],
+            a1s.at[target * HALVES + half],
+            a1r.at[p * HALVES + half],
+            c,
+            target,
+        ).start()
 
     def spread_pair(s, carry):
         pair = lax.rem(p // 2 + s, NB // 2)
@@ -265,22 +309,28 @@
         ).astype(bf16)
         for k in range(2):
             target = pair * 2 + k
-            block = rounded[k * FS : (k + 1) * FS]
-            spread[target] = block
+            for half in range(HALVES):
+                start = k * FS + half * HR
+                spread[target, half] = rounded[start : start + HR]
 
             @pl.when(target != p)
             def _():
-                remote(
-                    spread.at[target], rows_back.at[p], a1s.at[target], a1r.at[p], c, target
-                ).start()
+                send_rows(target, 0)
 
             @pl.when(target == p)
             def _():
-                rows_back[p] = block
+                rows_back[p] = spread[target]
 
         return carry
 
     lax.fori_loop(1, NB // 2 + 1, spread_pair, 0)
+    for half in range(1, HALVES):
+
+        def send_later(s, carry):
+            send_rows(lax.rem(p + s, NB), half)
+            return carry
+
+        lax.fori_loop(1, NB, send_later, 0)
 
     is_low = lane_low((E, FS))
     valid_up, valid_down = p > 0, p < NB - 1
@@ -316,81 +366,111 @@
     lax.fori_loop(0, 4, synth_pair, 0)
 
     top, mid, bottom = pl.ds(0, HALO), pl.ds(HALO, FS), pl.ds(HALO + FS, HALO)
-    first_half, second_half = pl.ds(0, HALO), pl.ds(HALO, HALO)
     every = slice(None)
     margin_copies = [
         remote(src, dst, h1s.at[k], h1r.at[k], a, b)
         for k, (src, dst, a, b) in enumerate(
             (
+                (syn_left.at[every, top], from_down_left, c, up),
+                (syn_left.at[every, bottom], from_up_left, c, down),
+                (syn_right.at[every, top], from_down_right, c, up),
+                (syn_right.at[every, bottom], from_up_right, c, down),
                 (syn.at[every, top], from_down, c, up),
                 (syn.at[every, bottom], from_up, c, down),
-                (syn_left.at[every, mid], from_right, left, p),
-                (syn_right.at[every, mid], from_left, right, p),
-                (syn_left.at[every, top], from_right_corner.at[every, second_half], left, up),
-                (syn_left.at[every, bottom], from_right_corner.at[every, first_half], left, down),
-                (syn_right.at[every, top], from_left_corner.at[every, second_half], right, up),
-                (syn_right.at[every, bottom], from_left_corner.at[every, first_half], right, down),
+                (fold_left, from_right, left, p),
+                (fold_right, from_left, right, p),
             )
         )
     ]
-    for copy in margin_copies:
+    for copy in margin_copies[:6]:
         copy.start()
 
-    acc[...] = jnp.zeros_like(acc)
-    for copy in table_copies:
+    for copy in turned_copies:
         copy.wait()
 
-    def back_block(s, carry):
-        j = lax.rem(p + s, NB)
-
-        @pl.when(s > 0)
-        def _():
-            remote(rows_back.at[j], rows_back.at[j], a1s.at[j], a1r.at[j], c, j).wait_recv()
-
-        block = rows_back[j]
-        start = pl.multiple_of(j * E, E)
-        for t in range(CHUNKS):
-            acc[t] += dot_nt(block, tables[t][:, pl.ds(start, E)])
-        return carry
-
-    lax.fori_loop(0, NB, back_block, 0)
-
-    for t in range(CHUNKS):
-        for k in range(2):
-            target = held[t] * 2 + k
-            adj_send[2 * t + k] = acc[t, :, k * E : (k + 1) * E].astype(bf16)
-
-            @pl.when(target != c)
-            def _():
-                remote(
-                    adj_send.at[2 * t + k], adj_recv.at[c], a2s.at[target], a2r.at[c], target, p
-                ).start()
-
-            @pl.when(target == c)
-            def _():
-                adj_recv[c] = adj_send[2 * t + k]
+    def back_half(half):
+        acc[...] = jnp.zeros_like(acc)
+
+        def back_group(s, carry):
+            g = lax.rem(p // GROUP + s, NB // GROUP)
+
+            def arrive(k, carry):
+                j = g * GROUP + k
+
+                @pl.when(j != p)
+                def _():
+                    index = j * HALVES + half
+                    block = rows_back.at[j, half]
+                    remote(block, block, a1s.at[index], a1r.at[index], c, j).wait_recv()
+
+                return carry
+
+            lax.fori_loop(0, GROUP, arrive, 0)
+            block = jnp.concatenate([rows_back[g * GROUP + k, half] for k in range(GROUP)], axis=1)
+            start = pl.multiple_of(g * GROUP * E, GROUP * E)
+            for t in range(CHUNKS):
+                lanes = slice(t * ROWS, (t + 1) * ROWS)
+                acc[t] += dot(block, turned_rows[pl.ds(start, GROUP * E), lanes])
+            return carry
+
+        lax.fori_loop(0, NB // GROUP, back_group, 0)
+        for target in range(C):
+            lanes = slice((target % 2) * E, (target % 2 + 1) * E)
+            adj_send[half, target] = acc[target // 2, :, lanes].astype(bf16)
+
+        def send_image(s, carry):
+            target = lax.rem(c + s, C)
+            remote(
+                adj_send.at[half, target],
+                adj_recv.at[half, c],
+                a2s.at[half * C + target],
+                a2r.at[half * C + c],
+                target,
+                p,
+            ).start()
+            return carry
+
+        lax.fori_loop(1, C, send_image, 0)
+        adj_recv[half, c] = adj_send[half, c]
+
+    back_half(0)
+
+    for copy in margin_copies[:4]:
+        copy.wait_recv()
+    row = lax.broadcasted_iota(jnp.int32, (FS, FS), 0)
+    side_ok = ((row < HALO) & valid_up) | ((row >= HALO) & valid_down)
+
+    def fold_edges(k, carry):
+        for own, above, below, out in (
+            (syn_left, from_up_left, from_down_left, fold_left),
+            (syn_right, from_up_right, from_down_right, fold_right),
+        ):
+            beside = jnp.concatenate([above[k], below[k]], axis=0).astype(f32)
+            total = own[k, HALO : HALO + FS].astype(f32) + jnp.where(side_ok, beside, 0.0)
+            out[k] = total.astype(bf16)
+        return carry
+
+    lax.fori_loop(0, 4, fold_edges, 0)
+    for copy in margin_copies[6:]:
+        copy.start()
+
+    for half in range(1, HALVES):
+        back_half(half)
 
     small[2].wait()
     small[3].wait()
     small[4].wait()
-    for copy in margin_copies:
+    for copy in margin_copies[4:]:
         copy.wait_recv()
     half_low = lane_low((FS, FS))
-    zero = jnp.zeros((), f32)
 
     def gather_prior(k, carry):
         pair = lax.rem(k, 4)
         is_first = k < 4
-        row = lax.broadcasted_iota(jnp.int32, (FS, FS), 0)
-        corner_ok = ((row < HALO) & valid_up) | ((row >= HALO) & valid_down)
-        sides = from_left[pair].astype(f32) + jnp.where(
-            corner_ok, from_left_corner[pair].astype(f32), 0.0
-        )
+        sides = from_left[pair].astype(f32)
         sides = jnp.where(is_first, sides, swap_halves(sides))
         tile0 = jnp.where(half_low & valid_left, sides, 0.0)
-        sides = from_right[pair].astype(f32) + jnp.where(
-            corner_ok, from_right_corner[pair].astype(f32), 0.0
-        )
+        sides = from_right[pair].astype(f32)
         sides = jnp.where(is_first, sides, swap_halves(sides))
         tile1 = jnp.where(jnp.logical_not(half_low) & valid_right, sides, 0.0)
         above = jnp.where(valid_up, from_up[k].astype(f32), 0.0)
@@ -403,32 +483,47 @@
 
     lax.fori_loop(0, C, gather_prior, 0)
 
-    def image_step(s, carry):
-        k = lax.rem(c + s, C)
-
-        @pl.when(s > 0)
-        def _():
-            remote(adj_recv.at[k], adj_recv.at[k], a2s.at[k], a2r.at[k], k, p).wait_recv()
-
-        updated = jnp.maximum(center[k] - step_size * adj_recv[k].astype(f32), 0.0)
-        tilde = 2.0 * updated - img[k]
-        center[k] = updated
-        padded[k, HALO : HALO + FS, :] = tilde.astype(bf16)
-        low[k] = low[k] + tilde
-
-        @pl.when(s > 0)
-        def _():
-            remote(
-                padded.at[k, mid], regrouped.at[c], a3s.at[k], a3r.at[c], k, p
-            ).start()
-
-        @pl.when(s == 0)
-        def _():
-            regrouped[c] = tilde.astype(bf16)
-
-        return carry
-
-    lax.fori_loop(0, C, image_step, 0)
+    def image_half(half):
+        inside = slice(half * HR, (half + 1) * HR)
+        here = pl.ds(HALO + half * HR, HR)
+
+        def image_step(s, carry):
+            k = lax.rem(c + s, C)
+
+            @pl.when(s > 0)
+            def _():
+                index = half * C + k
+                block = adj_recv.at[half, k]
+                remote(block, block, a2s.at[index], a2r.at[index], k, p).wait_recv()
+
+            adjoint = adj_recv[half, k].astype(f32)
+            updated = jnp.maximum(center[k, inside] - step_size * adjoint, 0.0)
+            tilde = 2.0 * updated - img[k, inside]
+            center[k, inside] = updated
+            padded[k, here] = tilde.astype(bf16)
+            low[k, inside] = low[k, inside] + tilde
+
+            @pl.when(s > 0)
+            def _():
+                remote(
+                    padded.at[k, here],
+                    regrouped.at[half, c],
+                    a3s.at[half * C + k],
+                    a3r.at[half * C + c],
+                    k,
+                    p,
+                ).start()
+
+            @pl.when(s == 0)
+            def _():
+                regrouped[half, c] = tilde.astype(bf16)
+
+            return carry
+
+        lax.fori_loop(0, C, image_step, 0)
+
+    for half in range(HALVES):
+        image_half(half)
     image_copy = pltpu.make_async_copy(center, image_out, out_sem.at[0])
     image_copy.start()
 
@@ -449,19 +544,68 @@
         remote(src, dst, h2s.at[k], h2r.at[k], a, b)
         for k, (src, dst, a, b) in enumerate(
             (
+                (edge_left, halo_right.at[every, mid], left, p),
+                (edge_right, halo_left.at[every, mid], right, p),
                 (padded.at[every, upper], padded.at[every, bottom], c, up),
                 (padded.at[every, lower], padded.at[every, top], c, down),
-                (edge_left, halo_right.at[every, mid], left, p),
-                (edge_right, halo_left.at[every, mid], right, p),
-                (edge_left.at[every, first_half], halo_right.at[every, bottom], left, up),
-                (edge_left.at[every, second_half], halo_right.at[every, top], left, down),
-                (edge_right.at[every, first_half], halo_left.at[every, bottom], right, up),
-                (edge_right.at[every, second_half], halo_left.at[every, top], right, down),
+                (halo_left.at[every, upper], halo_left.at[every, bottom], c, up),
+                (halo_left.at[every, lower], halo_left.at[every, top], c, down),
+                (halo_right.at[every, upper], halo_right.at[every, bottom], c, up),
+                (halo_right.at[every, lower], halo_right.at[every, top], c, down),
             )
         )
     ]
-    for copy in halo_copies:
+    for copy in halo_copies[:4]:
         copy.start()
+
+    def spectrum_half(half):
+        def arrive(s, carry):
+            k = lax.rem(c + s, C)
+            index = half * C + k
+            block = regrouped.at[half, k]
+            remote(block, block, a3s.at[index], a3r.at[index], k, p).wait_recv()
+            return carry
+
+        lax.fori_loop(1, C, arrive, 0)
+
+        def spectrum_block(s, carry):
+            j = lax.rem(p + s, NB)
+            start = pl.multiple_of(j * E, E)
+            total = None
+            for q in range(C):
+                rows_in = slice((q % 2) * E, (q % 2 + 1) * E)
+                term = dot(regrouped[half, q], tables[q // 2][rows_in, pl.ds(start, E)])
+                total = term if total is None else total + term
+            spec[half, j] = total.astype(bf16)
+
+            @pl.when(s < NB)
+            def _():
+                remote(
+                    spec.at[half, j],
+                    spec_recv.at[half, p],
+                    a4s.at[half * NB + j],
+                    a4r.at[half * NB + p],
+                    c,
+                    j,
+                ).start()
+
+            @pl.when(s == NB)
+            def _():
+                spec_recv[half, p] = total.astype(bf16)
+
+            return carry
+
+        lax.fori_loop(1, NB + 1, spectrum_block, 0)
+
+    for copy in table_copies:
+        copy.wait()
+    spectrum_half(0)
+    for copy in halo_copies[:2]:
+        copy.wait_recv()
+    for copy in halo_copies[4:]:
+        copy.start()
+    for half in range(1, HALVES):
+        spectrum_half(half)
 
     for f in range(2):
         lanes = slice(f * FS, (f + 1) * FS)
@@ -508,36 +652,7 @@
     low_copy = pltpu.make_async_copy(low_next, lowrank_out, low_out_sem.at[0])
     low_copy.start()
 
-    def arrive(s, carry):
-        k = lax.rem(c + s, C)
-        remote(regrouped.at[k], regrouped.at[k], a3s.at[k], a3r.at[k], k, p).wait_recv()
-        return carry
-
-    lax.fori_loop(1, C, arrive, 0)
-
-    def spectrum_block(s, carry):
-        j = lax.rem(p + s, NB)
-        start = pl.multiple_of(j * E, E)
-        total = None
-        for t in range(CHUNKS):
-            for k in range(2):
-                term = dot(regrouped[held[t] * 2 + k], tables[t][k * E : (k + 1) * E, pl.ds(start, E)])
-                total = term if total is None else total + term
-        spec[j] = total.astype(bf16)
-
-        @pl.when(s < NB)
-        def _():
-            remote(spec.at[j], spec_recv.at[p], a4s.at[j], a4r.at[p], c, j).start()
-
-        @pl.when(s == NB)
-        def _():
-            spec_recv[p] = total.astype(bf16)
-
-        return carry
-
-    lax.fori_loop(1, NB + 1, spectrum_block, 0)
-
-    for copy in halo_copies:
+    for copy in halo_copies[2:]:
         copy.wait_recv()
 
     def analysis(k, carry):
@@ -577,16 +692,23 @@
     row_copy.wait()
 
     def forward_block(s, carry):
-        j = lax.rem(p + s, NB)
-
-        @pl.when(s > 0)
-        def _():
-            remote(spec_recv.at[j], spec_recv.at[j], a4s.at[j], a4r.at[j], c, j).wait_recv()
-
-        block = spec_recv[j].astype(f32)
+        half = s // (NB // HALVES)
+        g = lax.rem(p // HALVES + s, NB // HALVES)
+        for b in range(HALVES):
+            j = g * HALVES + b
+
+            @pl.when(j != p)
+            def _():
+                index = half * NB + j
+                block = spec_recv.at[half, j]
+                remote(block, block, a4s.at[index], a4r.at[index], c, j).wait_recv()
+
+        block = jnp.concatenate(
+            [spec_recv[half, g * HALVES + b].astype(f32) for b in range(HALVES)], axis=0
+        )
         real = block[:, :BLK].reshape(FS // NB, NB, BLK)
         imag = block[:, BLK:].reshape(FS // NB, NB, BLK)
-        start = pl.multiple_of(j * E, E)
+        start = pl.multiple_of((g * HALVES + half) * E, E)
         rows_table = first_rows[:, pl.ds(start, E)]
         for q in range(R):
             cosine, sine = phases[q, 0][None], phases[q, 1][None]
@@ -616,14 +738,21 @@
 
     def end_facet(s, carry):
         j = lax.rem(p + s, NB)
-        remote(spec.at[j], spec_recv.at[j], a1s.at[j], a1r.at[j], c, j).wait_send()
-        remote(spec.at[j], spec_recv.at[j], a4s.at[j], a4r.at[j], c, j).wait_send()
+        for half in range(HALVES):
+            block = spec_recv.at[half, j]
+            sem = a1s.at[j * HALVES + half]
+            remote(block, block, sem, a1r.at[0], c, j).wait_send()
+            sem = a4s.at[half * NB + j]
+            remote(block, block, sem, a4r.at[0], c, j).wait_send()
         return carry
 
     def end_chan(s, carry):
         k = lax.rem(c + s, C)
-        remote(adj_send.at[k], adj_recv.at[k], a2s.at[k], a2r.at[k], k, p).wait_send()
-        remote(padded.at[k, mid], regrouped.at[k], a3s.at[k], a3r.at[k], k, p).wait_send()
+        for half in range(HALVES):
+            index = half * C + k
+            block = adj_recv.at[half, k]
+            remote(block, block, a2s.at[index], a2r.at[index], k, p).wait_send()
+            remote(block, block, a3s.at[index], a3r.at[index], k, p).wait_send()
         return carry
 
     lax.fori_loop(1, NB, end_facet, 0)
@@ -639,6 +768,30 @@
 
     lax.fori_loop(0, C, end_wavelet, 0)
     data_copy.wait()
+
+
+def hand_on(
+    image_in, low_in, wavelet_in, data_in, image_out, low_out, wavelet_out, data_out, *scratch
+):
+    image, low, wavelet, data, sem_in, sem_out = scratch
+    loads, stores = [], []
+    for src, held, dst in (
+        (wavelet_in, wavelet, wavelet_out),
+        (image_in, image, image_out),
+        (low_in, low, low_out),
+        (data_in, data, data_out),
+    ):
+        for k in range(src.shape[0]):
+            n = len(loads)
+            loads.append(pltpu.make_async_copy(src.at[k], held.at[k], sem_in.at[n]))
+            stores.append(pltpu.make_async_copy(held.at[k], dst.at[k], sem_out.at[n]))
+    for copy in loads:
+        copy.start()
+    for load, store in zip(loads, stores):
+        load.wait()
+        store.start()
+    for copy in stores:
+        copy.wait()
 
 
 def shards(
@@ -659,6 +812,7 @@
     scratch = (
         [vmem((ROWS, 2 * N), bf16)] * 4
         + [
+            vmem((2 * N, N), bf16),
             vmem((N, E), bf16),
             vmem((BLK, 2 * N), bf16),
             vmem((R, 2, NB, BLK), f32),
@@ -669,11 +823,11 @@
             vmem((2, rows, BLK), f32),
             vmem((rows, BLK), bf16),
             vmem((E, R * E), bf16),
-            vmem((NB, FS, E), bf16),
-            vmem((NB, FS, E), bf16),
-            vmem((CHUNKS, FS, ROWS), f32),
-            vmem((C, FS, E), bf16),
-            vmem((C, FS, E), bf16),
+            vmem((NB, HALVES, HR, E), bf16),
+            vmem((NB, HALVES, HR, E), bf16),
+            vmem((CHUNKS, HR, ROWS), f32),
+            vmem((HALVES, C, HR, E), bf16),
+            vmem((HALVES, C, HR, E), bf16),
             vmem((E, E), bf16),
             vmem((E, E), bf16),
             vmem((C, E, E), bf16),
@@ -682,6 +836,10 @@
             vmem((C, FS, E), f32),
             vmem((C, HALO, E), bf16),
             vmem((C, HALO, E), bf16),
+            vmem((4, HALO, FS), bf16),
+            vmem((4, HALO, FS), bf16),
+            vmem((4, HALO, FS), bf16),
+            vmem((4, HALO, FS), bf16),
             vmem((4, FS, FS), bf16),
             vmem((4, FS, FS), bf16),
             vmem((4, FS, FS), bf16),
@@ -691,27 +849,29 @@
             vmem((4, FS, FS), bf16),
             vmem((4, E, FS), bf16),
             vmem((4, E, FS), bf16),
-            vmem((C, FS, E), bf16),
-            vmem((NB, FS, E), bf16),
-            vmem((NB, FS, E), bf16),
+            vmem((HALVES, C, HR, E), bf16),
+            vmem((HALVES, NB, HR, E), bf16),
+            vmem((HALVES, NB, HR, E), bf16),
             vmem((rows, E), f32),
             vmem((C, C, FS), f32),
             vmem((C, C, FS), f32),
             vmem((C, FS, E), f32),
         ]
-        + [dma((n,)) for n in (4, 8, 7, 2, 8, 1, 16, 16, 8, 8, 8, 8, 16, 16, 8, 8, 8, 8)]
+        + [dma((n,)) for n in (4, 4, 8, 7, 2, 8, 1)
+            + (NB * HALVES,) * 2 + (C * HALVES,) * 4 + (NB * HALVES,) * 2 + (8,) * 4]
     )
     hbm = pl.BlockSpec(memory_space=pl.ANY)
     smem = pl.BlockSpec(memory_space=pltpu.SMEM)
-    image_next, lowrank_next, wavelet_next, data_next = pl.pallas_call(
+    result_shapes = (
+        jax.ShapeDtypeStruct((C, FS, E), f32),
+        jax.ShapeDtypeStruct((C, FS, E), f32),
+        jax.ShapeDtypeStruct((C, E, 2 * E), f32),
+        jax.ShapeDtypeStruct((2, rows, BLK), f32),
+    )
+    results = pl.pallas_call(
         body,
-        out_shape=(
-            jax.ShapeDtypeStruct((C, FS, E), f32),
-            jax.ShapeDtypeStruct((C, FS, E), f32),
-            jax.ShapeDtypeStruct((C, E, 2 * E), f32),
-            jax.ShapeDtypeStruct((2, rows, BLK), f32),
-        ),
-        in_specs=[smem] * 3 + [pl.BlockSpec(memory_space=pltpu.VMEM)] + [hbm] * 7,
+        out_shape=result_shapes,
+        in_specs=[smem] * 3 + [pl.BlockSpec(memory_space=pltpu.VMEM)] + [hbm] * 9,
         out_specs=(hbm,) * 4,
         scratch_shapes=scratch,
         compiler_params=pltpu.CompilerParams(
@@ -729,7 +889,18 @@
         observed.reshape(2, rows, BLK),
         kernel_weights.reshape(rows, BLK),
         jnp.asarray(dft_table()),
+        jnp.asarray(first_row_table()),
+        jnp.asarray(turned_table()),
     )
+    image_next, lowrank_next, wavelet_next, data_next = pl.pallas_call(
+        hand_on,
+        out_shape=result_shapes,
+        in_specs=[hbm] * 4,
+        out_specs=(hbm,) * 4,
+        scratch_shapes=[vmem(result.shape, f32) for result in result_shapes]
+        + [dma((3 * C + 2,))] * 2,
+        compiler_params=pltpu.CompilerParams(vmem_limit_bytes=60 * 1024 * 1024),
+    )(*results)
     return image_next, lowrank_next, wavelet_next, data_next.reshape(2, 1, rows, BLK)
 
 

time: 90.2 us -> 83.2 us (0.922)
  the two profiles are of different devices: /device:TPU:97 before, /device:TPU:0 now
where the time goes in v1:
time: 83.2 us; the launch traced here: 83 us
  Pallas kernels  81.7 us (98%)
  between operations  1.29 us (2%)
    pallas_call x1, Pallas kernels, shards(): pl.pallas_call(body, out_shape=result_shapes, in_specs=[smem] * 3 + [pl.B...  75.7 us
    pallas_call x1, Pallas kernels, shards(): pl.pallas_call(hand_on, out_shape=result_shapes, in_specs=[hbm] * 4, out_...  5.97 us

profile of v1, /device:TPU:0, one launch (start us, length us, event | category | flops | bytes accessed | tf_op | source)
XLA Modules:
  0.0 83.0 jit_solution(4431465350175837165)
XLA Ops:
  1.3 75.7 %shard_map.156 = (f32[8,128,256]{2,1,0:T(8,128)}, f32[8,128,256]{2,1,0:T(8,128)}, f32[8,256,512]{2,1,0:T(8,128)}, f32[2,512,128]{2,1,0:T(8,128)}) custom-call(s32[1,1,4]{2,1,0:T(1,128)} %rows_ref.1, s32[1,2]{1,0:T(1,128)} %widths_ref.1, f32[1,1]{1,0:T(1,128)S(6)} %copy.18.radii_ref, bf16[256,256]{1,0:T(8,128)(2,1)} %matrix_ref.1, f32[8,128,256]{2,1,0:T(8,128)} %image_hbm.1, ...), custom_call_target="tpu_custom_call" | custom-call | tf_op jit(solution)/shard_map/pallas_call | solution.py:871
  77.0 6.0 %shard_map.157 = (f32[8,128,256]{2,1,0:T(8,128)}, f32[8,128,256]{2,1,0:T(8,128)}, f32[8,256,512]{2,1,0:T(8,128)}, f32[2,512,128]{2,1,0:T(8,128)}) custom-call(f32[8,128,256]{2,1,0:T(8,128)} %get-tuple-element.12.image_in, f32[8,128,256]{2,1,0:T(8,128)} %get-tuple-element.13.low_in, f32[8,256,512]{2,1,0:T(8,128)} %get-tuple-element.14.wavelet_in, ...), custom_call_target="tpu_custom_call" | custom-call | tf_op jit(solution)/shard_map/pallas_call | solution.py:895

commit v2 on v1

--- a/solution.py
+++ b/solution.py
@@ -382,8 +382,33 @@
             )
         )
     ]
-    for copy in margin_copies[:6]:
-        copy.start()
+    to_up, to_down = (p > 0, p < NB - 1), (p < NB - 1, p > 0)
+    to_left, to_right = (c > 0, c < C - 1), (c < C - 1, c > 0)
+    margin_ends = [to_up, to_down] * 3 + [to_left, to_right]
+    halo_ends = [to_left, to_right] + [to_up, to_down] * 3
+
+    def start_some(copies, ends):
+        for copy, (sends, _) in zip(copies, ends):
+
+            @pl.when(sends)
+            def _():
+                copy.start()
+
+    def receive_some(copies, ends):
+        for copy, (_, receives) in zip(copies, ends):
+
+            @pl.when(receives)
+            def _():
+                copy.wait_recv()
+
+    def sent_some(copies, ends):
+        for copy, (sends, _) in zip(copies, ends):
+
+            @pl.when(sends)
+            def _():
+                copy.wait_send()
+
+    start_some(margin_copies[:6], margin_ends[:6])
 
     for copy in turned_copies:
         copy.wait()
@@ -435,8 +460,7 @@
 
     back_half(0)
 
-    for copy in margin_copies[:4]:
-        copy.wait_recv()
+    receive_some(margin_copies[:4], margin_ends[:4])
     row = lax.broadcasted_iota(jnp.int32, (FS, FS), 0)
     side_ok = ((row < HALO) & valid_up) | ((row >= HALO) & valid_down)
 
@@ -451,8 +475,7 @@
         return carry
 
     lax.fori_loop(0, 4, fold_edges, 0)
-    for copy in margin_copies[6:]:
-        copy.start()
+    start_some(margin_copies[6:], margin_ends[6:])
 
     for half in range(1, HALVES):
         back_half(half)
@@ -460,8 +483,7 @@
     small[2].wait()
     small[3].wait()
     small[4].wait()
-    for copy in margin_copies[4:]:
-        copy.wait_recv()
+    receive_some(margin_copies[4:], margin_ends[4:])
     half_low = lane_low((FS, FS))
 
     def gather_prior(k, carry):
@@ -555,8 +577,7 @@
             )
         )
     ]
-    for copy in halo_copies[:4]:
-        copy.start()
+    start_some(halo_copies[:4], halo_ends[:4])
 
     def spectrum_half(half):
         def arrive(s, carry):
@@ -600,10 +621,8 @@
     for copy in table_copies:
         copy.wait()
     spectrum_half(0)
-    for copy in halo_copies[:2]:
-        copy.wait_recv()
-    for copy in halo_copies[4:]:
-        copy.start()
+    receive_some(halo_copies[:2], halo_ends[:2])
+    start_some(halo_copies[4:], halo_ends[4:])
     for half in range(1, HALVES):
         spectrum_half(half)
 
@@ -652,8 +671,7 @@
     low_copy = pltpu.make_async_copy(low_next, lowrank_out, low_out_sem.at[0])
     low_copy.start()
 
-    for copy in halo_copies[2:]:
-        copy.wait_recv()
+    receive_some(halo_copies[2:], halo_ends[2:])
 
     def analysis(k, carry):
         pair = lax.rem(k, 4)
@@ -757,8 +775,7 @@
 
     lax.fori_loop(1, NB, end_facet, 0)
     lax.fori_loop(1, C, end_chan, 0)
-    for copy in margin_copies + halo_copies:
-        copy.wait_send()
+    sent_some(margin_copies + halo_copies, margin_ends + halo_ends)
     image_copy.wait()
     low_copy.wait()
 

time: 83.2 us -> 81.4 us (0.978)
  the two profiles are of different devices: /device:TPU:0 before, /device:TPU:10 now
where the time goes in v2:
time: 81.4 us; the launch traced here: 80.6 us
  Pallas kernels  79.3 us (97%)
  between operations  1.29 us (2%)
    pallas_call x1, Pallas kernels, shards(): pl.pallas_call(body, out_shape=result_shapes, in_specs=[smem] * 3 + [pl.B...  73.3 us
    pallas_call x1, Pallas kernels, shards(): pl.pallas_call(hand_on, out_shape=result_shapes, in_specs=[hbm] * 4, out_...  5.97 us

profile of v2, /device:TPU:10, one launch (start us, length us, event | category | flops | bytes accessed | tf_op | source)
XLA Modules:
  0.0 80.6 jit_solution(5000187835329516631)
XLA Ops:
  1.3 73.3 %shard_map.156 = (f32[8,128,256]{2,1,0:T(8,128)}, f32[8,128,256]{2,1,0:T(8,128)}, f32[8,256,512]{2,1,0:T(8,128)}, f32[2,512,128]{2,1,0:T(8,128)}) custom-call(s32[1,1,4]{2,1,0:T(1,128)} %rows_ref.1, s32[1,2]{1,0:T(1,128)} %widths_ref.1, f32[1,1]{1,0:T(1,128)S(6)} %copy.18.radii_ref, bf16[256,256]{1,0:T(8,128)(2,1)} %matrix_ref.1, f32[8,128,256]{2,1,0:T(8,128)} %image_hbm.1, ...), custom_call_target="tpu_custom_call" | custom-call | tf_op jit(solution)/shard_map/pallas_call | solution.py:888
  74.6 6.0 %shard_map.157 = (f32[8,128,256]{2,1,0:T(8,128)}, f32[8,128,256]{2,1,0:T(8,128)}, f32[8,256,512]{2,1,0:T(8,128)}, f32[2,512,128]{2,1,0:T(8,128)}) custom-call(f32[8,128,256]{2,1,0:T(8,128)} %get-tuple-element.12.image_in, f32[8,128,256]{2,1,0:T(8,128)} %get-tuple-element.13.low_in, f32[8,256,512]{2,1,0:T(8,128)} %get-tuple-element.14.wavelet_in, ...), custom_call_target="tpu_custom_call" | custom-call | tf_op jit(solution)/shard_map/pallas_call | solution.py:912
